TPU v7x, 32 devices: a whole 2x2x4 slice. The times are simulated.
32 devices in a mesh: bulk: 4 (over y, core), pair: 8 (over z, x).
Axes of the slice: x: 2, y: 2, z: 4, core: 2. Of those that a mesh axis runs over, the one named last changes fastest.
Arguments:
- spectra: float32 [1536, 2, 2048], P(('bulk', 'pair')), may hold values from -6 to 6
- pair_bin: int32 [2, 768, 48], P(None, ('bulk', 'pair')), may hold values from 0 to 127
Outputs:
- stacks: float32 [128, 1024], P(('bulk', 'pair'))
All inputs are finite; a program needn't handle non-finite values.
Results may differ from a plain program's by a relative error of at most 0.008.
Values may be sent and summed in bfloat16 or wider, within the bound.
A program may use at most 128 MiB of HBM per device.

v0:
```python
import functools
import math

import jax
import jax.numpy as jnp
import numpy as np
from jax import lax
from jax.experimental import pallas as pl
from jax.experimental.pallas import tpu as pltpu
from jax.sharding import PartitionSpec as P

FREQS = 2048
BAND_BINS = 32
LAGS = 1024
BIN_DEV = 4
GROUP = 4
LANES = 128
QUARTER = FREQS // GROUP
WIDTH = 256
CHUNKS = QUARTER // WIDTH
ROWS = GROUP * BIN_DEV
P_STEP = 48
F32 = jnp.float32
BF16 = jnp.bfloat16
MESH = pl.DeviceIdType.MESH


def lag_table():
    freq = np.arange(FREQS)[:, None]
    lag = np.arange(LAGS)[None, :] - LAGS // 2
    angle = (freq * lag % (2 * FREQS)) * (math.pi / FREQS)
    parts = [np.cos(angle), -np.sin(angle)]
    parts = [part.reshape(-1, 1, WIDTH, LAGS) for part in parts]
    return np.concatenate(parts, axis=1).reshape(-1, 2 * WIDTH, LAGS).astype(jnp.bfloat16)


def flat_bins(bin_in):
    rounds, rows, stations = bin_in.shape
    flat = rows * stations
    ids = jnp.concatenate([bin_in[rnd] for rnd in range(rounds)], axis=0)
    lane = lax.broadcasted_iota(jnp.int32, (1, flat), 1)
    row_of = lane // stations
    column = lane - row_of * stations
    spread = (lax.broadcasted_iota(jnp.int32, (stations, flat), 0) == column).astype(F32).astype(BF16)
    high, low = (ids // 16).astype(F32).astype(BF16), (ids % 16).astype(F32).astype(BF16)
    wide = 16.0 * jnp.dot(high, spread, preferred_element_type=F32)
    wide += jnp.dot(low, spread, preferred_element_type=F32)
    out = []
    for rnd in range(rounds):
        mine = lax.broadcasted_iota(jnp.int32, (rows, flat), 0) == row_of
        out.append(jnp.sum(jnp.where(mine, wide[rnd * rows : (rnd + 1) * rows], 0.0), axis=0, keepdims=True))
    return jnp.stack(out).astype(jnp.int32)


def kernel(
    n_bulk, n_pair, x_hbm, bin_hbm, table_ref, out_ref,
    x_ref, bin_in,
    own, met, lower, bins, hot, terms, total, part, share, counts, count_share, tab, lag, lag_share,
    x_send, x_recv, b_send, b_recv, s_send, s_recv, c_send, c_recv, l_send, l_recv, t_sem, in_sem,
):
    stations = x_ref.shape[0]
    n_mid = n_pair // GROUP
    groups = n_bulk * n_mid
    bulk, pair = lax.axis_index("bulk"), lax.axis_index("pair")
    side = pair // (n_pair // 2)
    across = pair % 2
    member = side * 2 + across
    mid = (pair // 2) % n_mid
    group = bulk * n_mid + mid

    def device(other_group, other_member):
        other_pair = (other_member // 2) * (n_pair // 2) + (other_group % n_mid) * 2 + other_member % 2
        return (other_group // n_mid, other_pair)

    def xor_member(step):
        flip_side, flip_x = step // 2, step % 2
        s = 1 - side if flip_side else side
        x = 1 - pair % 2 if flip_x else pair % 2
        return s * 2 + x

    def ring_group(step):
        return (group + step) % groups

    def back_group(step):
        return (group + groups - step) % groups

    inputs = [
        pltpu.make_async_copy(bin_hbm, bin_in, in_sem.at[0]),
        pltpu.make_async_copy(x_hbm, x_ref, in_sem.at[1]),
    ]
    for copy in inputs:
        copy.start()
    barrier = pltpu.get_barrier_semaphore()
    for step in range(1, GROUP):
        pl.semaphore_signal(barrier, inc=1, device_id=device(group, xor_member(step)), device_id_type=MESH)

    @pl.loop(1, groups)
    def _(step):
        pl.semaphore_signal(barrier, inc=1, device_id=device(ring_group(step), member), device_id_type=MESH)

    quarter_table = [
        pltpu.make_async_copy(table_ref.at[member * CHUNKS + c], tab.at[c], t_sem.at[c]) for c in range(CHUNKS)
    ]
    for copy in quarter_table:
        copy.start()

    def exchange(step, c):
        to = xor_member(step)
        return pltpu.make_async_remote_copy(
            own.at[c, to], met.at[c, member], x_send.at[step, c], x_recv.at[step, c],
            device_id=device(group, to), device_id_type=MESH,
        )

    def bin_exchange(step):
        return pltpu.make_async_remote_copy(
            bins.at[member], bins.at[member], b_send.at[step], b_recv.at[step],
            device_id=device(group, xor_member(step)), device_id_type=MESH,
        )

    band = lax.broadcasted_iota(jnp.int32, (LANES, LANES), 0) // BAND_BINS
    band_t = lax.broadcasted_iota(jnp.int32, (LANES, LANES), 1) // BAND_BINS
    average = jnp.where(band == band_t, 1.0 / BAND_BINS, 0.0).astype(BF16)

    for copy in inputs:
        copy.wait()
    bins[member] = flat_bins(bin_in)

    for c in range(CHUNKS):
        for tile in range(WIDTH // LANES):
            spots = [q * QUARTER + c * WIDTH + tile * LANES for q in range(GROUP)]
            real = jnp.concatenate([x_ref[:, 0, at : at + LANES] for at in spots], axis=0)
            imag = jnp.concatenate([x_ref[:, 1, at : at + LANES] for at in spots], axis=0)
            power = real * real + imag * imag
            high = power.astype(BF16)
            low = (power - high.astype(F32)).astype(BF16)
            band_power = jnp.dot(high, average, preferred_element_type=F32)
            band_power += jnp.dot(low, average, preferred_element_type=F32)
            scale = lax.rsqrt(band_power + 1e-06)
            real, imag = (real * scale).astype(BF16), (imag * scale).astype(BF16)
            at = tile * LANES
            for q in range(GROUP):
                own[c, q, :, at : at + LANES] = real[q * stations : (q + 1) * stations]
                own[c, q, :, WIDTH + at : WIDTH + at + LANES] = imag[q * stations : (q + 1) * stations]
        if c == 0:
            pl.semaphore_wait(barrier, GROUP - 1 + groups - 1)
            for step in (1, 2, 3):
                bin_exchange(step).start()
        for step in (1, 2, 3):
            exchange(step, c).start()
        met[c, member] = own[c, member]

    for step in (1, 2, 3):
        bin_exchange(step).wait()

    n_rows = groups * ROWS
    row = lax.broadcasted_iota(jnp.int32, (n_rows, LANES), 0)
    row_group, row_member = row // ROWS, (row // BIN_DEV) % GROUP
    row_pair = (row_member // 2) * (n_pair // 2) + (row_group % n_mid) * 2 + row_member % 2
    row_bin = ((row_group // n_mid) * n_pair + row_pair) * BIN_DEV + row % BIN_DEV

    meets = ((0, 2, 0), (1, 3, 0), (0, 1, 1), (2, 3, 1))
    width = P_STEP * stations
    steps = stations // P_STEP
    seen = jnp.zeros((n_rows, LANES), F32)
    for m, (lo, up, rnd) in enumerate(meets):
        half = bins.shape[-1]
        for tile in range(2 * half // LANES):
            at = tile * LANES
            ids = bins[lo if at < half else up, rnd, :, at % half : at % half + LANES]
            chosen = jnp.where(row_bin == ids, 1.0, 0.0)
            seen += chosen
            hot[m * steps + at // width, :, at % width : at % width + LANES] = chosen.astype(BF16)
    seen = jnp.sum(seen, axis=1, keepdims=True)
    counts[...] = jnp.broadcast_to(seen, (n_rows, LANES)).reshape(groups, ROWS, LANES)

    def count_copy(step):
        return pltpu.make_async_remote_copy(
            counts.at[ring_group(step)], count_share.at[step], c_send.at[step], c_recv.at[step],
            device_id=device(ring_group(step), member), device_id_type=MESH,
        )

    @pl.loop(1, groups)
    def _(step):
        count_copy(step).start()

    def stack(c, meet, lo, up):
        up_real, up_imag = met[c, up, :, :WIDTH], met[c, up, :, WIDTH:]
        sums = None
        for k in range(steps):
            for i in range(P_STEP):
                p = k * P_STEP + i
                lo_real = jnp.broadcast_to(lower[lo, p : p + 1, :WIDTH], (stations, WIDTH)).astype(BF16)
                lo_imag = jnp.broadcast_to(lower[lo, p : p + 1, WIDTH:], (stations, WIDTH)).astype(BF16)
                at = slice(p * stations, (p + 1) * stations)
                terms[at, :WIDTH] = lo_real * up_real + lo_imag * up_imag
                terms[at, WIDTH:] = lo_imag * up_real - lo_real * up_imag
            got = jnp.dot(
                hot[meet * steps + k], terms[k * width : (k + 1) * width, :], preferred_element_type=F32
            )
            sums = got if sums is None else sums + got
        return sums

    @pl.loop(0, CHUNKS)
    def _(c):
        exchange(1, c).wait_recv()
        lower[side * 2] = met[c, side * 2].astype(F32)
        total[c] = stack(c, 2 + side, side * 2, side * 2 + 1)

    def share_copy(c, step):
        return pltpu.make_async_remote_copy(
            part.at[c, ring_group(step)], share.at[c, step], s_send.at[c, step], s_recv.at[c, step],
            device_id=device(ring_group(step), member), device_id_type=MESH,
        )

    @pl.loop(0, CHUNKS)
    def _(c):
        exchange(2, c).wait_recv()

        @pl.loop(0, 3)
        def _(j):
            @pl.when(j == 1)
            def _():
                exchange(3, c).wait_recv()

            column = (across + j) % 2
            meet = jnp.where(j == 2, 3 - side, column)
            lo = jnp.where(j == 2, 2 - side * 2, column)
            up = jnp.where(j == 2, 3 - side * 2, column + 2)
            lower[lo] = met[c, lo].astype(F32)
            total[c] += stack(c, meet, lo, up)

        part[c] = total[c].astype(BF16).reshape(groups, ROWS, 2 * WIDTH)

        @pl.loop(1, groups)
        def _(step):
            share_copy(c, step).start()

    @pl.loop(1, groups)
    def _(step):
        count_copy(step).wait()

    count = counts[group]
    for step in range(1, groups):
        count += count_share[step]
    norm = lax.rsqrt(jnp.maximum(count[:, :1], 1.0)) / math.sqrt(FREQS)

    lags = None
    for c in range(CHUNKS):
        @pl.loop(1, groups)
        def _(step):
            share_copy(c, step).wait()

        stacked = part[c, group].astype(F32)
        for step in range(1, groups):
            stacked += share[c, step].astype(F32)
        quarter_table[c].wait()
        got = jnp.dot(stacked.astype(BF16), tab[c], preferred_element_type=F32)
        lags = got if lags is None else lags + got
    lags = lags * norm
    for m in range(GROUP):
        lag[m] = lags[m * BIN_DEV : (m + 1) * BIN_DEV]

    def lag_copy(step):
        to = xor_member(step)
        return pltpu.make_async_remote_copy(
            lag.at[to], lag_share.at[step], l_send.at[step], l_recv.at[step],
            device_id=device(group, to), device_id_type=MESH,
        )

    for step in (2, 3, 1):
        lag_copy(step).start()
    for step in (1, 2, 3):
        for c in range(CHUNKS):
            exchange(step, c).wait_send()
    result = lag[member]
    for step in (1, 2, 3):
        lag_copy(step).wait()
        result += lag_share[step]
    out_ref[...] = result


def body(table, n_bulk, n_pair, spectra, pair_bin):
    stations = spectra.shape[0]
    rounds = pair_bin.shape[0]
    groups = n_bulk * n_pair // GROUP
    n_rows = groups * ROWS
    half = pair_bin.shape[1] * pair_bin.shape[2]
    steps = stations // P_STEP
    dma = pltpu.SemaphoreType.DMA
    return pl.pallas_call(
        functools.partial(kernel, n_bulk, n_pair),
        out_shape=jax.ShapeDtypeStruct((BIN_DEV, LAGS), F32),
        in_specs=[
            pl.BlockSpec(memory_space=pltpu.HBM),
            pl.BlockSpec(memory_space=pltpu.HBM),
            pl.BlockSpec(memory_space=pltpu.HBM),
        ],
        out_specs=pl.BlockSpec(memory_space=pltpu.VMEM),
        scratch_shapes=[
            pltpu.VMEM(spectra.shape, F32),
            pltpu.VMEM(pair_bin.shape, jnp.int32),
            pltpu.VMEM((CHUNKS, GROUP, stations, 2 * WIDTH), BF16),
            pltpu.VMEM((CHUNKS, GROUP, stations, 2 * WIDTH), BF16),
            pltpu.VMEM((GROUP - 1, stations, 2 * WIDTH), F32),
            pltpu.VMEM((GROUP, rounds, 1, half), jnp.int32),
            pltpu.VMEM((GROUP * steps, n_rows, P_STEP * stations), BF16),
            pltpu.VMEM((stations * stations, 2 * WIDTH), BF16),
            pltpu.VMEM((CHUNKS, n_rows, 2 * WIDTH), F32),
            pltpu.VMEM((CHUNKS, groups, ROWS, 2 * WIDTH), BF16),
            pltpu.VMEM((CHUNKS, groups, ROWS, 2 * WIDTH), BF16),
            pltpu.VMEM((groups, ROWS, LANES), F32),
            pltpu.VMEM((groups, ROWS, LANES), F32),
            pltpu.VMEM((CHUNKS, 2 * WIDTH, LAGS), BF16),
            pltpu.VMEM((GROUP, BIN_DEV, LAGS), F32),
            pltpu.VMEM((GROUP, BIN_DEV, LAGS), F32),
            dma((GROUP, CHUNKS)), dma((GROUP, CHUNKS)),
            dma((GROUP,)), dma((GROUP,)),
            dma((CHUNKS, groups)), dma((CHUNKS, groups)),
            dma((groups,)), dma((groups,)),
            dma((GROUP,)), dma((GROUP,)),
            dma((CHUNKS,)),
            dma((2,)),
        ],
        compiler_params=pltpu.CompilerParams(
            collective_id=0, has_side_effects=True, vmem_limit_bytes=56203673
        ),
    )(spectra, pair_bin, jnp.asarray(table))


def solution(mesh):
    return jax.shard_map(
        functools.partial(body, lag_table(), mesh.shape["bulk"], mesh.shape["pair"]),
        mesh=mesh,
        in_specs=(P(("bulk", "pair"), None, None), P(None, ("bulk", "pair"), None)),
        out_specs=P(("bulk", "pair"), None),
        check_vma=False,
    )
```

profile of v0, /device:TPU:0, one launch (start us, length us, event | category | flops | bytes accessed | tf_op | source)
XLA Modules:
  0.0 28.8 jit_solution(3696998909815135097)
XLA Ops:
  0.0 0.0 copy-start
  0.0 0.7 %copy-done = s32[2,24,48]{2,1,0:T(8,128)S(1)} copy-done((s32[2,24,48]{2,1,0:T(8,128)S(1)}, s32[2,24,48]{2,1,0:T(8,128)}, u32[]{:S(2)}) %copy-start) | copy-done | bytes 9240
  0.7 27.4 %shard_map.37 = f32[4,1024]{1,0:T(4,128)S(1)} custom-call(f32[48,2,2048]{2,1,0:T(2,128)} %x_hbm.1, s32[2,24,48]{2,1,0:T(8,128)S(1)} %copy-done, bf16[8,512,1024]{2,1,0:T(8,128)(2,1)} %constant.2.clone.table_ref), custom_call_target="tpu_custom_call" | custom-call | tf_op jit(solution)/shard_map/pallas_call | solution.py:290
  28.2 0.6 %copy.5 = f32[4,1024]{1,0:T(4,128)} copy(f32[4,1024]{1,0:T(4,128)S(1)} %shard_map.37) | data formatting | bytes 32768
Async XLA Ops:
  0.0 0.7 %copy-start = (s32[2,24,48]{2,1,0:T(8,128)S(1)}, s32[2,24,48]{2,1,0:T(8,128)}, u32[]{:S(2)}) copy-start(s32[2,24,48]{2,1,0:T(8,128)} %bin_hbm.1) | copy-start | bytes 27652
where the time goes:
time: 29 us; the launch traced here: 28.8 us
  Pallas kernels  27.4 us (94%)
  local copies, waits for them, and re-layouts  1.34 us (5%)
    pallas_call x1, Pallas kernels, body(): pl.pallas_call(functools.partial(kernel, n_bulk, n_pair), out_shape=jax.S...  27.4 us
    unnamed x3, local copies, waits for them, and re-layouts  1.34 us

commit v1 on v0

--- a/solution.py
+++ b/solution.py
@@ -56,7 +56,7 @@
     n_bulk, n_pair, x_hbm, bin_hbm, table_ref, out_ref,
     x_ref, bin_in,
     own, met, lower, bins, hot, terms, total, part, share, counts, count_share, tab, lag, lag_share,
-    x_send, x_recv, b_send, b_recv, s_send, s_recv, c_send, c_recv, l_send, l_recv, t_sem, in_sem,
+    x_send, x_recv, b_send, b_recv, s_send, s_recv, c_send, c_recv, l_send, l_recv, t_sem, in_sem, relay,
 ):
     stations = x_ref.shape[0]
     n_mid = n_pair // GROUP
@@ -91,12 +91,14 @@
     for copy in inputs:
         copy.start()
     barrier = pltpu.get_barrier_semaphore()
-    for step in range(1, GROUP):
-        pl.semaphore_signal(barrier, inc=1, device_id=device(group, xor_member(step)), device_id_type=MESH)
-
-    @pl.loop(1, groups)
-    def _(step):
-        pl.semaphore_signal(barrier, inc=1, device_id=device(ring_group(step), member), device_id_type=MESH)
+    bits = [1 << k for k in range(groups.bit_length() - 1)]
+
+    def flip_group(bit):
+        return device(group + bit - 2 * bit * ((group // bit) % 2), member)
+
+    neighbours = [device(group, xor_member(step)) for step in (1, 2)] + [flip_group(bit) for bit in bits]
+    for near in neighbours:
+        pl.semaphore_signal(barrier, inc=1, device_id=near, device_id_type=MESH)
 
     quarter_table = [
         pltpu.make_async_copy(table_ref.at[member * CHUNKS + c], tab.at[c], t_sem.at[c]) for c in range(CHUNKS)
@@ -142,13 +144,25 @@
                 own[c, q, :, at : at + LANES] = real[q * stations : (q + 1) * stations]
                 own[c, q, :, WIDTH + at : WIDTH + at + LANES] = imag[q * stations : (q + 1) * stations]
         if c == 0:
-            pl.semaphore_wait(barrier, GROUP - 1 + groups - 1)
-            for step in (1, 2, 3):
+            pl.semaphore_wait(barrier, len(neighbours))
+            pl.semaphore_signal(relay.at[0], inc=1, device_id=device(group, xor_member(1)), device_id_type=MESH)
+            pl.semaphore_signal(relay.at[1], inc=1, device_id=flip_group(bits[0]), device_id_type=MESH)
+            exchange(2, c).start()
+            for step in (2, 1):
                 bin_exchange(step).start()
-        for step in (1, 2, 3):
-            exchange(step, c).start()
+            exchange(1, c).start()
+            pl.semaphore_wait(relay.at[0], 1)
+            bin_exchange(3).start()
+            exchange(3, c).start()
+        else:
+            for step in (3, 2, 1):
+                exchange(step, c).start()
         met[c, member] = own[c, member]
 
+    for k in range(1, len(bits)):
+        pl.semaphore_wait(relay.at[k], 1)
+        if k + 1 < len(bits):
+            pl.semaphore_signal(relay.at[k + 1], inc=1, device_id=flip_group(bits[k]), device_id_type=MESH)
     for step in (1, 2, 3):
         bin_exchange(step).wait()
 
@@ -320,9 +334,10 @@
             dma((GROUP,)), dma((GROUP,)),
             dma((CHUNKS,)),
             dma((2,)),
+            pltpu.SemaphoreType.REGULAR((max(1, groups.bit_length() - 1),)),
         ],
         compiler_params=pltpu.CompilerParams(
-            collective_id=0, has_side_effects=True, vmem_limit_bytes=56203673
+            collective_id=0, has_side_effects=True, vmem_limit_bytes=56529919
         ),
     )(spectra, pair_bin, jnp.asarray(table))
 

time: 29 us -> 28.7 us (0.990)
  local copies, waits for them, and re-layouts: 1.34 us -> 0.61 us
  Pallas kernels: 27.4 us -> 27.9 us
    unnamed x3 -> x1, local copies, waits for them, and re-layouts: 1.34 us -> 0.61 us
    pallas_call x1, Pallas kernels: 27.4 us -> 27.9 us  [body(): pl.pallas_call(functools.partial(kernel, n_bulk, n_pair), out_shape=jax.S...]
where the time goes in v1:
time: 28.7 us; the launch traced here: 28.6 us
  Pallas kernels  27.9 us (97%)
  local copies, waits for them, and re-layouts  0.61 us (2%)
    pallas_call x1, Pallas kernels, body(): pl.pallas_call(functools.partial(kernel, n_bulk, n_pair), out_shape=jax.S...  27.9 us
    unnamed x1, local copies, waits for them, and re-layouts  0.61 us

profile of v1, /device:TPU:0, one launch (start us, length us, event | category | flops | bytes accessed | tf_op | source)
XLA Modules:
  0.0 28.6 jit_solution(10562540340664475214)
XLA Ops:
  0.0 27.9 %shard_map.37 = f32[4,1024]{1,0:T(4,128)S(1)} custom-call(f32[48,2,2048]{2,1,0:T(2,128)} %x_hbm.1, s32[2,24,48]{2,1,0:T(8,128)} %bin_hbm.1, bf16[8,512,1024]{2,1,0:T(8,128)(2,1)} %constant.2.clone.table_ref), custom_call_target="tpu_custom_call" | custom-call | tf_op jit(solution)/shard_map/pallas_call | solution.py:304
  28.0 0.6 %copy.5 = f32[4,1024]{1,0:T(4,128)} copy(f32[4,1024]{1,0:T(4,128)S(1)} %shard_map.37) | data formatting | bytes 32768

commit v2 on v0

v2 whole, which is shorter than its diff:
```python
import functools
import math

import jax
import jax.numpy as jnp
import numpy as np
from jax import lax
from jax.experimental import pallas as pl
from jax.experimental.pallas import tpu as pltpu
from jax.sharding import PartitionSpec as P

FREQS = 2048
BAND_BINS = 32
LAGS = 1024
BIN_DEV = 4
GROUP = 4
LANES = 128
WIDTH = 256
COLS = 2 * WIDTH
SPAN = 2 * WIDTH
CHUNKS = FREQS // SPAN
TILES = COLS // LANES
F32 = jnp.float32
BF16 = jnp.bfloat16
MESH = pl.DeviceIdType.MESH


def lag_table():
    freq = np.arange(FREQS)[:, None]
    lag = np.arange(LAGS)[None, :] - LAGS // 2
    angle = (freq * lag % (2 * FREQS)) * (math.pi / FREQS)
    parts = [np.cos(angle), -np.sin(angle)]
    parts = [part.reshape(CHUNKS, 2, WIDTH, LAGS) for part in parts]
    return np.concatenate(parts, axis=2).astype(jnp.bfloat16)


def flat_bins(bin_in):
    rounds, rows, stations = bin_in.shape
    flat = rows * stations
    ids = jnp.concatenate([bin_in[rnd] for rnd in range(rounds)], axis=0)
    lane = lax.broadcasted_iota(jnp.int32, (1, flat), 1)
    row_of = lane // stations
    column = lane - row_of * stations
    spread = (lax.broadcasted_iota(jnp.int32, (stations, flat), 0) == column).astype(F32).astype(BF16)
    high, low = (ids // 16).astype(F32).astype(BF16), (ids % 16).astype(F32).astype(BF16)
    wide = 16.0 * jnp.dot(high, spread, preferred_element_type=F32)
    wide += jnp.dot(low, spread, preferred_element_type=F32)
    out = []
    for rnd in range(rounds):
        mine = lax.broadcasted_iota(jnp.int32, (rows, flat), 0) == row_of
        out.append(jnp.sum(jnp.where(mine, wide[rnd * rows : (rnd + 1) * rows], 0.0), axis=0, keepdims=True))
    return jnp.stack(out).astype(jnp.int32)


def kernel(
    n_bulk, n_pair, x_hbm, bin_hbm, table_hbm, out_ref,
    x_ref, bin_in, own, met, lower, bins, hot, terms, total, kept, give, got, part, share,
    counts, count_got, count_part, count_share, tab,
    x_send, x_recv, b_send, b_recv, g_send, g_recv, s_send, s_recv, c_send, c_recv, t_sem, in_sem, relay,
):
    stations = x_ref.shape[0]
    n_mid = n_pair // GROUP
    spots = n_bulk // 2 * n_mid
    peers = GROUP * spots
    n_half = peers * BIN_DEV
    bulk, pair = lax.axis_index("bulk"), lax.axis_index("pair")
    core = bulk % 2
    side = pair // (n_pair // 2)
    across = pair % 2
    half = side + across - 2 * side * across
    member = side * 2 + across
    spot = bulk // 2 * n_mid + (pair // 2) % n_mid

    def place(some_spot, some_member):
        some_pair = some_member // 2 * (n_pair // 2) + some_spot % n_mid * 2 + some_member % 2
        return some_spot // n_mid * 2 + core, some_pair

    def xor_member(step):
        flip_side, flip_x = step // 2, step % 2
        s = side + flip_side - 2 * side * flip_side
        x = across + flip_x - 2 * across * flip_x
        return s * 2 + x

    def flip_spot(bit):
        return place(spot + bit - 2 * bit * (spot // bit % 2), member)

    twin = (bulk + 1 - 2 * core, pair)
    beside, beyond = place(spot, xor_member(1)), place(spot, xor_member(2))
    links = [flip_spot(1 << k) for k in range(spots.bit_length() - 1)]

    spans = [
        pltpu.make_async_copy(
            x_hbm.at[:, :, pl.ds(c * SPAN, SPAN)], x_ref.at[:, :, pl.ds(c * SPAN, SPAN)], in_sem.at[1 + c]
        )
        for c in range(CHUNKS)
    ]
    bins_in = pltpu.make_async_copy(bin_hbm, bin_in, in_sem.at[0])
    spans[0].start()
    bins_in.start()
    for copy in spans[1:]:
        copy.start()
    barrier = pltpu.get_barrier_semaphore()
    neighbours = [beyond, beside, twin] + links
    for near in neighbours:
        pl.semaphore_signal(barrier, inc=1, device_id=near, device_id_type=MESH)
    tables = [pltpu.make_async_copy(table_hbm.at[c], tab.at[c], t_sem.at[c]) for c in range(CHUNKS)]
    for copy in tables:
        copy.start()

    def exchange(step, c):
        return pltpu.make_async_remote_copy(
            own.at[c, 1 - half], met.at[c, step], x_send.at[step, c], x_recv.at[step, c],
            device_id=beyond if step == 2 else beside, device_id_type=MESH,
        )

    def bin_exchange(step):
        return pltpu.make_async_remote_copy(
            bins.at[2 - step], bins.at[4 - step], b_send.at[step], b_recv.at[step],
            device_id=beyond if step == 2 else beside, device_id_type=MESH,
        )

    band = lax.broadcasted_iota(jnp.int32, (LANES, LANES), 0) // BAND_BINS
    band_t = lax.broadcasted_iota(jnp.int32, (LANES, LANES), 1) // BAND_BINS
    average = jnp.where(band == band_t, 1.0 / BAND_BINS, 0.0).astype(BF16)

    def whiten(c):
        spans[c].wait()
        starts = [c * SPAN + at for at in range(0, SPAN, LANES)]
        real = jnp.concatenate([x_ref[:, 0, at : at + LANES] for at in starts], axis=0)
        imag = jnp.concatenate([x_ref[:, 1, at : at + LANES] for at in starts], axis=0)
        power = real * real + imag * imag
        high = power.astype(BF16)
        low = (power - high.astype(F32)).astype(BF16)
        band_power = jnp.dot(high, average, preferred_element_type=F32)
        band_power += jnp.dot(low, average, preferred_element_type=F32)
        scale = lax.rsqrt(band_power + 1e-06)
        real, imag = (real * scale).astype(BF16), (imag * scale).astype(BF16)
        for tile in range(SPAN // LANES):
            q, at = tile * LANES // WIDTH, tile * LANES % WIDTH
            rows = slice(tile * stations, (tile + 1) * stations)
            own[c, q, :, at : at + LANES] = real[rows]
            own[c, q, :, WIDTH + at : WIDTH + at + LANES] = imag[rows]

    whiten(0)
    bins_in.wait()
    bins[:2] = flat_bins(bin_in)
    pl.semaphore_wait(barrier, len(neighbours))
    pl.semaphore_signal(relay.at[0], inc=1, device_id=beside, device_id_type=MESH)
    for step in (2, 1):
        bin_exchange(step).start()
    for c in range(CHUNKS):
        if c > 0:
            whiten(c)
        for step in (2, 1):
            exchange(step, c).start()
    met[:, 0] = own[:, half]

    n_rows = 2 * n_half
    row = lax.broadcasted_iota(jnp.int32, (n_rows, LANES), 0)
    row_half, row_in = row // n_half, row % n_half
    row_peer = row_in // BIN_DEV % 2 * (peers // 2) + row_in // (2 * BIN_DEV)
    row_member, row_spot = row_peer // spots, (spot + row_peer % spots) % spots
    row_side, row_across = row_member // 2, row_member % 2
    row_side = side + row_side - 2 * side * row_side
    row_across = across + row_across - 2 * across * row_across
    row_core = core + row_half - 2 * core * row_half
    row_pair = row_side * (n_pair // 2) + row_spot % n_mid * 2 + row_across
    row_bin = ((row_spot // n_mid * 2 + row_core) * n_pair + row_pair) * BIN_DEV + row % BIN_DEV

    for k in range(len(links) + 1):
        pl.semaphore_wait(relay.at[k], 1)
        if k < len(links):
            pl.semaphore_signal(relay.at[k + 1], inc=1, device_id=links[k], device_id_type=MESH)

    seen = jnp.zeros((n_rows, LANES), F32)
    flat = bins.shape[-1]
    for rnd, is_up in ((1, across), (0, side)):
        bin_exchange(2 - rnd).wait()
        for tile in range(2 * flat // LANES):
            at = tile * LANES
            slot = rnd + 2 * is_up if at < flat else rnd + 2 - 2 * is_up
            ids = bins[slot, :, at % flat : at % flat + LANES]
            chosen = jnp.where(row_bin == ids, 1.0, 0.0)
            seen += chosen
            hot[rnd, :, at : at + LANES] = chosen.astype(BF16)
    seen = jnp.sum(seen, axis=1, keepdims=True)
    counts[...] = jnp.broadcast_to(seen, (n_rows, LANES)).reshape(2, peers // 2, 2 * BIN_DEV, LANES)

    count_swap = pltpu.make_async_remote_copy(
        counts.at[1], count_got, g_send.at[CHUNKS], g_recv.at[CHUNKS], device_id=twin, device_id_type=MESH
    )
    count_swap.start()

    def count_copy(block):
        to = place((spot + block % spots) % spots, xor_member(block // spots * 3))
        return pltpu.make_async_remote_copy(
            count_part.at[block], count_share.at[block], c_send.at[block], c_recv.at[block],
            device_id=to, device_id_type=MESH,
        )

    def stack(c, rnd, is_up):
        partner = 2 - rnd
        lo, up = partner * is_up, partner - partner * is_up
        up_real, up_imag = met[c, up, :, :WIDTH], met[c, up, :, WIDTH:]
        lower[...] = met[c, lo].astype(F32)
        for p in range(stations):
            lo_real = jnp.broadcast_to(lower[p : p + 1, :WIDTH], (stations, WIDTH)).astype(BF16)
            lo_imag = jnp.broadcast_to(lower[p : p + 1, WIDTH:], (stations, WIDTH)).astype(BF16)
            at = slice(p * stations, (p + 1) * stations)
            terms[at, :WIDTH] = lo_real * up_real + lo_imag * up_imag
            terms[at, WIDTH:] = lo_imag * up_real - lo_real * up_imag
        return jnp.dot(hot[rnd], terms[...], preferred_element_type=F32)

    @pl.loop(0, CHUNKS)
    def _(c):
        exchange(1, c).wait_recv()
        total[c] = stack(c, 1, across)

    count_swap.wait()
    count_part[...] = counts[0] + count_got[...]
    for block in range(1, 2 * spots):
        count_copy(block).start()

    def swap(c):
        return pltpu.make_async_remote_copy(
            give.at[c], got.at[c], g_send.at[c], g_recv.at[c], device_id=twin, device_id_type=MESH
        )

    def share_copy(c, peer):
        to = place((spot + peer % spots) % spots, xor_member(peer // spots))
        return pltpu.make_async_remote_copy(
            part.at[c, peer], share.at[c, peer], s_send.at[c, peer], s_recv.at[c, peer],
            device_id=to, device_id_type=MESH,
        )

    first_rows = lax.broadcasted_iota(jnp.int32, (n_half, LANES), 0) % (2 * BIN_DEV) < BIN_DEV

    def finish(c):
        swap(c).wait_recv()
        sums = kept[c] + got[c].astype(F32)
        even, odd = [], []
        for at in range(0, COLS, 2 * LANES):
            first, second = sums[:, at : at + LANES], sums[:, at + LANES : at + 2 * LANES]
            picked = jnp.where(first_rows, first, pltpu.roll(second, BIN_DEV, 0))
            even.append(picked.reshape(peers // 2, 2 * BIN_DEV, LANES))
            picked = jnp.where(first_rows, pltpu.roll(first, n_half - BIN_DEV, 0), second)
            odd.append(picked.reshape(peers // 2, 2 * BIN_DEV, LANES))
        part[c, : peers // 2] = jnp.concatenate(even, axis=1).astype(BF16)
        part[c, peers // 2 :] = jnp.concatenate(odd, axis=1).astype(BF16)

        @pl.loop(1, peers)
        def _(back):
            share_copy(c, peers - back).start()

    @pl.loop(0, CHUNKS)
    def _(c):
        exchange(2, c).wait_recv()
        sums = total[c] + stack(c, 0, side)
        kept[c] = sums[:n_half]
        give[c] = sums[n_half:].astype(BF16)
        swap(c).start()

        @pl.when(c > 0)
        def _():
            finish(c - 1)

    finish(CHUNKS - 1)

    for block in range(1, 2 * spots):
        count_copy(block).wait()
    count = jnp.zeros((BIN_DEV, LANES), F32)
    for block in range(2 * spots):
        piece = count_share[block] if block else count_part[0]
        count += piece[:BIN_DEV] if block < spots else piece[BIN_DEV:]
    norm = lax.rsqrt(jnp.maximum(count[:, :1], 1.0)) / math.sqrt(FREQS)
    for c in range(CHUNKS):
        for step in (1, 2):
            exchange(step, c).wait_send()
        swap(c).wait_send()

    lags = jnp.zeros((BIN_DEV, LAGS), F32)
    for c in range(CHUNKS):
        tables[c].wait()

        @pl.loop(1, peers)
        def _(peer):
            share_copy(c, peer).wait()

        for which, steps in ((half, (0, 3)), (1 - half, (1, 2))):
            stacked = None
            for step in steps:
                for near in range(spots):
                    peer = step * spots + near
                    piece = (share if peer else part)[c, peer].astype(F32)
                    stacked = piece if stacked is None else stacked + piece
            stacked = jnp.concatenate([stacked[at : at + BIN_DEV] for at in range(0, TILES * BIN_DEV, BIN_DEV)], axis=1)
            lags += jnp.dot(stacked.astype(BF16), tab[c, which], preferred_element_type=F32)
    out_ref[...] = lags * norm


def body(table, n_bulk, n_pair, spectra, pair_bin):
    stations = spectra.shape[0]
    spots = n_bulk * n_pair // (2 * GROUP)
    peers = GROUP * spots
    n_half = peers * BIN_DEV
    flat = pair_bin.shape[1] * pair_bin.shape[2]
    dma = pltpu.SemaphoreType.DMA
    return pl.pallas_call(
        functools.partial(kernel, n_bulk, n_pair),
        out_shape=jax.ShapeDtypeStruct((BIN_DEV, LAGS), F32),
        in_specs=[pl.BlockSpec(memory_space=pltpu.HBM)] * 3,
        out_specs=pl.BlockSpec(memory_space=pltpu.VMEM),
        scratch_shapes=[
            pltpu.VMEM(spectra.shape, F32),
            pltpu.VMEM(pair_bin.shape, jnp.int32),
            pltpu.VMEM((CHUNKS, 2, stations, COLS), BF16),
            pltpu.VMEM((CHUNKS, 3, stations, COLS), BF16),
            pltpu.VMEM((stations, COLS), F32),
            pltpu.VMEM((4, 1, flat), jnp.int32),
            pltpu.VMEM((2, 2 * n_half, 2 * flat), BF16),
            pltpu.VMEM((2 * flat, COLS), BF16),
            pltpu.VMEM((CHUNKS, 2 * n_half, COLS), F32),
            pltpu.VMEM((CHUNKS, n_half, COLS), F32),
            pltpu.VMEM((CHUNKS, n_half, COLS), BF16),
            pltpu.VMEM((CHUNKS, n_half, COLS), BF16),
            pltpu.VMEM((CHUNKS, peers, TILES * BIN_DEV, LANES), BF16),
            pltpu.VMEM((CHUNKS, peers, TILES * BIN_DEV, LANES), BF16),
            pltpu.VMEM((2, peers // 2, 2 * BIN_DEV, LANES), F32),
            pltpu.VMEM((peers // 2, 2 * BIN_DEV, LANES), F32),
            pltpu.VMEM((peers // 2, 2 * BIN_DEV, LANES), F32),
            pltpu.VMEM((peers // 2, 2 * BIN_DEV, LANES), F32),
            pltpu.VMEM((CHUNKS, 2, COLS, LAGS), BF16),
            dma((3, CHUNKS)), dma((3, CHUNKS)),
            dma((3,)), dma((3,)),
            dma((CHUNKS + 1,)), dma((CHUNKS + 1,)),
            dma((CHUNKS, peers)), dma((CHUNKS, peers)),
            dma((2 * spots,)), dma((2 * spots,)),
            dma((CHUNKS,)),
            dma((1 + CHUNKS,)),
            pltpu.SemaphoreType.REGULAR((spots.bit_length(),)),
        ],
        compiler_params=pltpu.CompilerParams(
            collective_id=0, has_side_effects=True, vmem_limit_bytes=56529919
        ),
    )(spectra, pair_bin, jnp.asarray(table))


def solution(mesh):
    return jax.shard_map(
        functools.partial(body, lag_table(), mesh.shape["bulk"], mesh.shape["pair"]),
        mesh=mesh,
        in_specs=(P(("bulk", "pair"), None, None), P(None, ("bulk", "pair"), None)),
        out_specs=P(("bulk", "pair"), None),
        check_vma=False,
    )
```

time: 29 us -> 26.5 us (0.914)
  Pallas kernels: 27.4 us -> 25.7 us
  local copies, waits for them, and re-layouts: 1.34 us -> 0.61 us
    pallas_call x1, Pallas kernels: 27.4 us -> 25.7 us  [body(): pl.pallas_call(functools.partial(kernel, n_bulk, n_pair), out_shape=jax.S...]
    unnamed x3 -> x1, local copies, waits for them, and re-layouts: 1.34 us -> 0.61 us
where the time goes in v2:
time: 26.5 us; the launch traced here: 26.4 us
  Pallas kernels  25.7 us (97%)
  local copies, waits for them, and re-layouts  0.61 us (2%)
    pallas_call x1, Pallas kernels, body(): pl.pallas_call(functools.partial(kernel, n_bulk, n_pair), out_shape=jax.S...  25.7 us
    unnamed x1, local copies, waits for them, and re-layouts  0.61 us

profile of v2, /device:TPU:0, one launch (start us, length us, event | category | flops | bytes accessed | tf_op | source)
XLA Modules:
  0.0 26.4 jit_solution(13062212423949183487)
XLA Ops:
  0.0 25.7 %shard_map.37 = f32[4,1024]{1,0:T(4,128)S(1)} custom-call(f32[48,2,2048]{2,1,0:T(2,128)} %x_hbm.1, s32[2,24,48]{2,1,0:T(8,128)} %bin_hbm.1, bf16[4,2,512,1024]{3,2,1,0:T(8,128)(2,1)} %constant.2.clone.table_hbm), custom_call_target="tpu_custom_call" | custom-call | tf_op jit(solution)/shard_map/pallas_call | solution.py:308
  25.8 0.6 %copy.5 = f32[4,1024]{1,0:T(4,128)} copy(f32[4,1024]{1,0:T(4,128)S(1)} %shard_map.37) | data formatting | bytes 32768

commit v3 on v2

--- a/solution.py
+++ b/solution.py
@@ -56,11 +56,12 @@
     n_bulk, n_pair, x_hbm, bin_hbm, table_hbm, out_ref,
     x_ref, bin_in, own, met, lower, bins, hot, terms, total, kept, give, got, part, share,
     counts, count_got, count_part, count_share, tab,
-    x_send, x_recv, b_send, b_recv, g_send, g_recv, s_send, s_recv, c_send, c_recv, t_sem, in_sem, relay,
+    sent, x_recv, b_recv, g_recv, s_send, s_recv, c_recv, in_sem, relay,
 ):
     stations = x_ref.shape[0]
     n_mid = n_pair // GROUP
-    spots = n_bulk // 2 * n_mid
+    n_y = n_bulk // 2
+    spots = n_y * n_mid
     peers = GROUP * spots
     n_half = peers * BIN_DEV
     bulk, pair = lax.axis_index("bulk"), lax.axis_index("pair")
@@ -103,19 +104,18 @@
     neighbours = [beyond, beside, twin] + links
     for near in neighbours:
         pl.semaphore_signal(barrier, inc=1, device_id=near, device_id_type=MESH)
-    tables = [pltpu.make_async_copy(table_hbm.at[c], tab.at[c], t_sem.at[c]) for c in range(CHUNKS)]
-    for copy in tables:
-        copy.start()
+    tables = pltpu.make_async_copy(table_hbm, tab, in_sem.at[1 + CHUNKS])
+    tables.start()
 
     def exchange(step, c):
         return pltpu.make_async_remote_copy(
-            own.at[c, 1 - half], met.at[c, step], x_send.at[step, c], x_recv.at[step, c],
+            own.at[c, 1 - half], met.at[c, step], sent.at[0], x_recv.at[step - 1, c],
             device_id=beyond if step == 2 else beside, device_id_type=MESH,
         )
 
     def bin_exchange(step):
         return pltpu.make_async_remote_copy(
-            bins.at[2 - step], bins.at[4 - step], b_send.at[step], b_recv.at[step],
+            bins.at[2 - step], bins.at[4 - step], sent.at[1], b_recv.at[step - 1],
             device_id=beyond if step == 2 else beside, device_id_type=MESH,
         )
 
@@ -175,7 +175,7 @@
     seen = jnp.zeros((n_rows, LANES), F32)
     flat = bins.shape[-1]
     for rnd, is_up in ((1, across), (0, side)):
-        bin_exchange(2 - rnd).wait()
+        bin_exchange(2 - rnd).wait_recv()
         for tile in range(2 * flat // LANES):
             at = tile * LANES
             slot = rnd + 2 * is_up if at < flat else rnd + 2 - 2 * is_up
@@ -187,14 +187,14 @@
     counts[...] = jnp.broadcast_to(seen, (n_rows, LANES)).reshape(2, peers // 2, 2 * BIN_DEV, LANES)
 
     count_swap = pltpu.make_async_remote_copy(
-        counts.at[1], count_got, g_send.at[CHUNKS], g_recv.at[CHUNKS], device_id=twin, device_id_type=MESH
+        counts.at[1], count_got, sent.at[2], g_recv.at[CHUNKS - 1], device_id=twin, device_id_type=MESH
     )
     count_swap.start()
 
     def count_copy(block):
         to = place((spot + block % spots) % spots, xor_member(block // spots * 3))
         return pltpu.make_async_remote_copy(
-            count_part.at[block], count_share.at[block], c_send.at[block], c_recv.at[block],
+            count_part.at[block], count_share.at[block], sent.at[3], c_recv.at[0],
             device_id=to, device_id_type=MESH,
         )
 
@@ -223,36 +223,59 @@
 
     def swap(c):
         return pltpu.make_async_remote_copy(
-            give.at[c], got.at[c], g_send.at[c], g_recv.at[c], device_id=twin, device_id_type=MESH
-        )
-
-    def share_copy(c, peer):
-        to = place((spot + peer % spots) % spots, xor_member(peer // spots))
-        return pltpu.make_async_remote_copy(
-            part.at[c, peer], share.at[c, peer], s_send.at[c, peer], s_recv.at[c, peer],
-            device_id=to, device_id_type=MESH,
-        )
+            give.at[c], got.at[c], sent.at[4], g_recv.at[c], device_id=twin, device_id_type=MESH
+        )
+
+    def share_starts(c, other_core):
+        for i in range(peers):
+            far_side, far_mid = i // (peers // 2), i // (2 * n_y) % n_mid
+            far_spot, far_across = i // 2 % n_y * n_mid + far_mid, i % 2
+            flip_side = side + far_side - 2 * side * far_side
+            flip_x = across + far_across - 2 * across * far_across
+            peer = (flip_side * 2 + flip_x) * spots + (far_spot + spots - spot) % spots
+            far_pair = far_side * (n_pair // 2) + far_mid * 2 + far_across
+
+            def copy(at, far_core):
+                return pltpu.make_async_remote_copy(
+                    part.at[at, peer], share.at[at, peer], s_send.at[at], s_recv.at[at],
+                    device_id=(far_spot // n_mid * 2 + far_core, far_pair), device_id_type=MESH,
+                )
+
+            @pl.when(peer > 0)
+            def _():
+                copy(c, core).start()
+
+            if other_core:
+                copy(c + 1, 1 - core).start()
+
+    def share_wait(at, first):
+        whole = pltpu.make_async_remote_copy(
+            part.at[at, pl.ds(first, peers - first)], share.at[at, pl.ds(first, peers - first)],
+            s_send.at[at], s_recv.at[at], device_id=twin, device_id_type=MESH,
+        )
+        whole.wait()
 
     first_rows = lax.broadcasted_iota(jnp.int32, (n_half, LANES), 0) % (2 * BIN_DEV) < BIN_DEV
 
-    def finish(c):
-        swap(c).wait_recv()
-        sums = kept[c] + got[c].astype(F32)
+    def pack(at, sums):
         even, odd = [], []
-        for at in range(0, COLS, 2 * LANES):
-            first, second = sums[:, at : at + LANES], sums[:, at + LANES : at + 2 * LANES]
+        for col in range(0, COLS, 2 * LANES):
+            first, second = sums[:, col : col + LANES], sums[:, col + LANES : col + 2 * LANES]
             picked = jnp.where(first_rows, first, pltpu.roll(second, BIN_DEV, 0))
             even.append(picked.reshape(peers // 2, 2 * BIN_DEV, LANES))
             picked = jnp.where(first_rows, pltpu.roll(first, n_half - BIN_DEV, 0), second)
             odd.append(picked.reshape(peers // 2, 2 * BIN_DEV, LANES))
-        part[c, : peers // 2] = jnp.concatenate(even, axis=1).astype(BF16)
-        part[c, peers // 2 :] = jnp.concatenate(odd, axis=1).astype(BF16)
-
-        @pl.loop(1, peers)
-        def _(back):
-            share_copy(c, peers - back).start()
-
-    @pl.loop(0, CHUNKS)
+        part[at, : peers // 2] = jnp.concatenate(even, axis=1).astype(BF16)
+        part[at, peers // 2 :] = jnp.concatenate(odd, axis=1).astype(BF16)
+
+    def finish(c):
+        swap(c).wait_recv()
+        pack(c, kept[c] + got[c].astype(F32))
+        share_starts(c, False)
+
+    last = CHUNKS - 1
+
+    @pl.loop(0, last)
     def _(c):
         exchange(2, c).wait_recv()
         sums = total[c] + stack(c, 0, side)
@@ -264,35 +287,46 @@
         def _():
             finish(c - 1)
 
-    finish(CHUNKS - 1)
-
-    for block in range(1, 2 * spots):
-        count_copy(block).wait()
+    finish(last - 1)
+    exchange(2, last).wait_recv()
+    sums = total[last] + stack(last, 0, side)
+    pack(last, sums[:n_half])
+    pack(last + 1, sums[n_half:])
+    share_starts(last, True)
+
+    pltpu.make_async_remote_copy(
+        bins.at[pl.ds(0, 2)], bins.at[pl.ds(2, 2)], sent.at[1], b_recv.at[0], device_id=twin, device_id_type=MESH
+    ).wait_send()
+    pltpu.make_async_remote_copy(
+        own, own, sent.at[0], x_recv.at[0, 0], device_id=twin, device_id_type=MESH
+    ).wait_send()
+    pltpu.make_async_remote_copy(
+        give, got, sent.at[4], g_recv.at[0], device_id=twin, device_id_type=MESH
+    ).wait_send()
+    rest = pl.ds(1, 2 * spots - 1)
+    pltpu.make_async_remote_copy(
+        count_part.at[rest], count_share.at[rest], sent.at[3], c_recv.at[0], device_id=twin, device_id_type=MESH
+    ).wait()
     count = jnp.zeros((BIN_DEV, LANES), F32)
     for block in range(2 * spots):
         piece = count_share[block] if block else count_part[0]
         count += piece[:BIN_DEV] if block < spots else piece[BIN_DEV:]
     norm = lax.rsqrt(jnp.maximum(count[:, :1], 1.0)) / math.sqrt(FREQS)
+
+    lags = jnp.zeros((BIN_DEV, LAGS), F32)
+    tables.wait()
     for c in range(CHUNKS):
-        for step in (1, 2):
-            exchange(step, c).wait_send()
-        swap(c).wait_send()
-
-    lags = jnp.zeros((BIN_DEV, LAGS), F32)
-    for c in range(CHUNKS):
-        tables[c].wait()
-
-        @pl.loop(1, peers)
-        def _(peer):
-            share_copy(c, peer).wait()
-
+        share_wait(c, 1)
+        if c == last:
+            share_wait(c + 1, 0)
         for which, steps in ((half, (0, 3)), (1 - half, (1, 2))):
             stacked = None
-            for step in steps:
-                for near in range(spots):
-                    peer = step * spots + near
-                    piece = (share if peer else part)[c, peer].astype(F32)
-                    stacked = piece if stacked is None else stacked + piece
+            for at in (c, c + 1)[: 2 if c == last else 1]:
+                for step in steps:
+                    for near in range(spots):
+                        peer = step * spots + near
+                        piece = (share if peer or at > c else part)[at, peer].astype(F32)
+                        stacked = piece if stacked is None else stacked + piece
             stacked = jnp.concatenate([stacked[at : at + BIN_DEV] for at in range(0, TILES * BIN_DEV, BIN_DEV)], axis=1)
             lags += jnp.dot(stacked.astype(BF16), tab[c, which], preferred_element_type=F32)
     out_ref[...] = lags * norm
@@ -320,23 +354,23 @@
             pltpu.VMEM((2, 2 * n_half, 2 * flat), BF16),
             pltpu.VMEM((2 * flat, COLS), BF16),
             pltpu.VMEM((CHUNKS, 2 * n_half, COLS), F32),
-            pltpu.VMEM((CHUNKS, n_half, COLS), F32),
-            pltpu.VMEM((CHUNKS, n_half, COLS), BF16),
-            pltpu.VMEM((CHUNKS, n_half, COLS), BF16),
-            pltpu.VMEM((CHUNKS, peers, TILES * BIN_DEV, LANES), BF16),
-            pltpu.VMEM((CHUNKS, peers, TILES * BIN_DEV, LANES), BF16),
+            pltpu.VMEM((CHUNKS - 1, n_half, COLS), F32),
+            pltpu.VMEM((CHUNKS - 1, n_half, COLS), BF16),
+            pltpu.VMEM((CHUNKS - 1, n_half, COLS), BF16),
+            pltpu.VMEM((CHUNKS + 1, peers, TILES * BIN_DEV, LANES), BF16),
+            pltpu.VMEM((CHUNKS + 1, peers, TILES * BIN_DEV, LANES), BF16),
             pltpu.VMEM((2, peers // 2, 2 * BIN_DEV, LANES), F32),
             pltpu.VMEM((peers // 2, 2 * BIN_DEV, LANES), F32),
             pltpu.VMEM((peers // 2, 2 * BIN_DEV, LANES), F32),
             pltpu.VMEM((peers // 2, 2 * BIN_DEV, LANES), F32),
             pltpu.VMEM((CHUNKS, 2, COLS, LAGS), BF16),
-            dma((3, CHUNKS)), dma((3, CHUNKS)),
-            dma((3,)), dma((3,)),
+            dma((5,)),
+            dma((2, CHUNKS)),
+            dma((2,)),
+            dma((CHUNKS,)),
             dma((CHUNKS + 1,)), dma((CHUNKS + 1,)),
-            dma((CHUNKS, peers)), dma((CHUNKS, peers)),
-            dma((2 * spots,)), dma((2 * spots,)),
-            dma((CHUNKS,)),
-            dma((1 + CHUNKS,)),
+            dma((1,)),
+            dma((2 + CHUNKS,)),
             pltpu.SemaphoreType.REGULAR((spots.bit_length(),)),
         ],
         compiler_params=pltpu.CompilerParams(

time: 26.5 us -> 24.4 us (0.921)
  Pallas kernels: 25.7 us -> 23.6 us
    pallas_call x1, Pallas kernels: 25.7 us -> 23.6 us  [body(): pl.pallas_call(functools.partial(kernel, n_bulk, n_pair), out_shape=jax.S...]
where the time goes in v3:
time: 24.4 us; the launch traced here: 24.3 us
  Pallas kernels  23.6 us (97%)
  local copies, waits for them, and re-layouts  0.61 us (2%)
    pallas_call x1, Pallas kernels, body(): pl.pallas_call(functools.partial(kernel, n_bulk, n_pair), out_shape=jax.S...  23.6 us
    unnamed x1, local copies, waits for them, and re-layouts  0.61 us

profile of v3, /device:TPU:0, one launch (start us, length us, event | category | flops | bytes accessed | tf_op | source)
XLA Modules:
  0.0 24.3 jit_solution(18069318112561750662)
XLA Ops:
  0.0 23.6 %shard_map.37 = f32[4,1024]{1,0:T(4,128)S(1)} custom-call(f32[48,2,2048]{2,1,0:T(2,128)} %x_hbm.1, s32[2,24,48]{2,1,0:T(8,128)} %bin_hbm.1, bf16[4,2,512,1024]{3,2,1,0:T(8,128)(2,1)} %constant.2.clone.table_hbm), custom_call_target="tpu_custom_call" | custom-call | tf_op jit(solution)/shard_map/pallas_call | solution.py:342
  23.7 0.6 %copy.5 = f32[4,1024]{1,0:T(4,128)} copy(f32[4,1024]{1,0:T(4,128)S(1)} %shard_map.37) | data formatting | bytes 32768

commit v4 on v3

--- a/solution.py
+++ b/solution.py
@@ -89,6 +89,10 @@
     beside, beyond = place(spot, xor_member(1)), place(spot, xor_member(2))
     links = [flip_spot(1 << k) for k in range(spots.bit_length() - 1)]
 
+    barrier = pltpu.get_barrier_semaphore()
+    neighbours = [beyond, beside, twin] + links
+    for near in neighbours:
+        pl.semaphore_signal(barrier, inc=1, device_id=near, device_id_type=MESH)
     spans = [
         pltpu.make_async_copy(
             x_hbm.at[:, :, pl.ds(c * SPAN, SPAN)], x_ref.at[:, :, pl.ds(c * SPAN, SPAN)], in_sem.at[1 + c]
@@ -100,10 +104,6 @@
     bins_in.start()
     for copy in spans[1:]:
         copy.start()
-    barrier = pltpu.get_barrier_semaphore()
-    neighbours = [beyond, beside, twin] + links
-    for near in neighbours:
-        pl.semaphore_signal(barrier, inc=1, device_id=near, device_id_type=MESH)
     tables = pltpu.make_async_copy(table_hbm, tab, in_sem.at[1 + CHUNKS])
     tables.start()
 
@@ -122,6 +122,8 @@
     band = lax.broadcasted_iota(jnp.int32, (LANES, LANES), 0) // BAND_BINS
     band_t = lax.broadcasted_iota(jnp.int32, (LANES, LANES), 1) // BAND_BINS
     average = jnp.where(band == band_t, 1.0 / BAND_BINS, 0.0).astype(BF16)
+
+    prompt = (side == 1) | ((pair // 2) % n_mid >= n_mid // 2)
 
     def whiten(c):
         spans[c].wait()
@@ -151,8 +153,11 @@
     for c in range(CHUNKS):
         if c > 0:
             whiten(c)
-        for step in (2, 1):
-            exchange(step, c).start()
+        if c < 2:
+            exchange(2, c).start()
+        else:
+            pl.when(prompt)(exchange(2, c).start)
+        exchange(1, c).start()
     met[:, 0] = own[:, half]
 
     n_rows = 2 * n_half
@@ -186,6 +191,11 @@
     seen = jnp.sum(seen, axis=1, keepdims=True)
     counts[...] = jnp.broadcast_to(seen, (n_rows, LANES)).reshape(2, peers // 2, 2 * BIN_DEV, LANES)
 
+    @pl.when(jnp.logical_not(prompt))
+    def _():
+        for c in range(2, CHUNKS):
+            exchange(2, c).start()
+
     count_swap = pltpu.make_async_remote_copy(
         counts.at[1], count_got, sent.at[2], g_recv.at[CHUNKS - 1], device_id=twin, device_id_type=MESH
     )
@@ -226,7 +236,7 @@
             give.at[c], got.at[c], sent.at[4], g_recv.at[c], device_id=twin, device_id_type=MESH
         )
 
-    def share_starts(c, other_core):
+    def share_starts(c, other_core, before=None):
         for i in range(peers):
             far_side, far_mid = i // (peers // 2), i // (2 * n_y) % n_mid
             far_spot, far_across = i // 2 % n_y * n_mid + far_mid, i % 2
@@ -243,6 +253,8 @@
 
             @pl.when(peer > 0)
             def _():
+                if before is not None:
+                    copy(before, core).start()
                 copy(c, core).start()
 
             if other_core:
@@ -287,12 +299,13 @@
         def _():
             finish(c - 1)
 
-    finish(last - 1)
+    swap(last - 1).wait_recv()
+    pack(last - 1, kept[last - 1] + got[last - 1].astype(F32))
     exchange(2, last).wait_recv()
     sums = total[last] + stack(last, 0, side)
     pack(last, sums[:n_half])
     pack(last + 1, sums[n_half:])
-    share_starts(last, True)
+    share_starts(last, True, last - 1)
 
     pltpu.make_async_remote_copy(
         bins.at[pl.ds(0, 2)], bins.at[pl.ds(2, 2)], sent.at[1], b_recv.at[0], device_id=twin, device_id_type=MESH

time: 24.4 us -> 23.4 us (0.959)
  Pallas kernels: 23.6 us -> 22.6 us
    pallas_call x1, Pallas kernels: 23.6 us -> 22.6 us  [body(): pl.pallas_call(functools.partial(kernel, n_bulk, n_pair), out_shape=jax.S...]
where the time goes in v4:
time: 23.4 us; the launch traced here: 23.2 us
  Pallas kernels  22.6 us (97%)
  local copies, waits for them, and re-layouts  0.61 us (3%)
    pallas_call x1, Pallas kernels, body(): pl.pallas_call(functools.partial(kernel, n_bulk, n_pair), out_shape=jax.S...  22.6 us
    unnamed x1, local copies, waits for them, and re-layouts  0.61 us

profile of v4, /device:TPU:0, one launch (start us, length us, event | category | flops | bytes accessed | tf_op | source)
XLA Modules:
  0.0 23.2 jit_solution(7075412566032700935)
XLA Ops:
  0.0 22.6 %shard_map.37 = f32[4,1024]{1,0:T(4,128)S(1)} custom-call(f32[48,2,2048]{2,1,0:T(2,128)} %x_hbm.1, s32[2,24,48]{2,1,0:T(8,128)} %bin_hbm.1, bf16[4,2,512,1024]{3,2,1,0:T(8,128)(2,1)} %constant.2.clone.table_hbm), custom_call_target="tpu_custom_call" | custom-call | tf_op jit(solution)/shard_map/pallas_call | solution.py:355
  22.6 0.6 %copy.5 = f32[4,1024]{1,0:T(4,128)} copy(f32[4,1024]{1,0:T(4,128)S(1)} %shard_map.37) | data formatting | bytes 32768

commit v5 on v4

--- a/solution.py
+++ b/solution.py
@@ -239,7 +239,7 @@
     def share_starts(c, other_core, before=None):
         for i in range(peers):
             far_side, far_mid = i // (peers // 2), i // (2 * n_y) % n_mid
-            far_spot, far_across = i // 2 % n_y * n_mid + far_mid, i % 2
+            far_spot, far_across = i % n_y * n_mid + far_mid, i // n_y % 2
             flip_side = side + far_side - 2 * side * far_side
             flip_x = across + far_across - 2 * across * far_across
             peer = (flip_side * 2 + flip_x) * spots + (far_spot + spots - spot) % spots

time: 23.4 us -> 23.4 us (level)
  no operation moved by 1% of the time
where the time goes in v5:
time: 23.4 us; the launch traced here: 23.2 us
  Pallas kernels  22.6 us (97%)
  local copies, waits for them, and re-layouts  0.61 us (3%)
    pallas_call x1, Pallas kernels, body(): pl.pallas_call(functools.partial(kernel, n_bulk, n_pair), out_shape=jax.S...  22.6 us
    unnamed x1, local copies, waits for them, and re-layouts  0.61 us

profile of v5, /device:TPU:0, one launch (start us, length us, event | category | flops | bytes accessed | tf_op | source)
XLA Modules:
  0.0 23.2 jit_solution(1731208565710437826)
XLA Ops:
  0.0 22.6 %shard_map.37 = f32[4,1024]{1,0:T(4,128)S(1)} custom-call(f32[48,2,2048]{2,1,0:T(2,128)} %x_hbm.1, s32[2,24,48]{2,1,0:T(8,128)} %bin_hbm.1, bf16[4,2,512,1024]{3,2,1,0:T(8,128)(2,1)} %constant.2.clone.table_hbm), custom_call_target="tpu_custom_call" | custom-call | tf_op jit(solution)/shard_map/pallas_call | solution.py:355
  22.6 0.6 %copy.5 = f32[4,1024]{1,0:T(4,128)} copy(f32[4,1024]{1,0:T(4,128)S(1)} %shard_map.37) | data formatting | bytes 32768
